TPU v7x, 256 devices: a whole 4x4x8 slice. The times are simulated.
256 devices in a mesh: row: 2 (over core), col: 16 (over y, x), depth: 8 (over z).
Axes of the slice: x: 4, y: 4, z: 8, core: 2. Of those that a mesh axis runs over, the one named last changes fastest.
Arguments:
- tensor: bfloat16 [4096, 128, 2048], P(('row', 'col', 'depth')), may hold values from -6 to 6
- density: bfloat16 [4096, 1024], P(('row', 'col', 'depth')), may hold values from -0.09375 to 0.09375
- tensor_mask: int32 [64, 2, 32], replicated, may hold values 0 or 1
- density_mask: int32 [64, 16], replicated, may hold values 0 or 1
Outputs:
- contracted: bfloat16 [1024, 128, 2048], P('depth', 'row', 'col')
All inputs are finite; a program needn't handle non-finite values.
Results may differ from a plain program's by a relative error of at most 0.017.
Values may be sent and summed in bfloat16 or wider, within the bound.
A program may use at most 192 MiB of HBM per device.

v0:
```python
import jax
import jax.numpy as jnp
from jax import lax
from jax.sharding import PartitionSpec as P

BLK = 64


def body(tensor, density, tensor_mask, density_mask):
    nu_dev, mu_total, aux_total = tensor.shape
    sigma_total = density.shape[1]
    n_dep = lax.axis_size("depth")
    first_row = lax.axis_index(("row", "col", "depth")) * nu_dev
    row_keep = lax.dynamic_slice_in_dim(jnp.repeat(tensor_mask, BLK, axis=0), first_row, nu_dev, 0)
    shaped = tensor.reshape(nu_dev, mu_total // BLK, BLK, aux_total // BLK, BLK)
    tensor_kept = (shaped * row_keep[:, :, None, :, None].astype(tensor.dtype)).reshape(
        nu_dev, mu_total, aux_total
    )
    density_keep = lax.dynamic_slice_in_dim(
        jnp.repeat(density_mask, BLK, axis=0), first_row, nu_dev, 0
    )
    density_kept = (
        density.reshape(nu_dev, sigma_total // BLK, BLK)
        * density_keep[:, :, None].astype(density.dtype)
    ).reshape(nu_dev, sigma_total)
    density_all = lax.all_gather(density_kept, ("row", "col"), axis=0, tiled=True)
    by_aux = lax.all_to_all(tensor_kept, "col", split_axis=2, concat_axis=0, tiled=True)
    remapped = lax.all_to_all(by_aux, "row", split_axis=1, concat_axis=0, tiled=True)
    mu_local = remapped.shape[1]
    aux_local = remapped.shape[2]
    flattened = remapped.reshape(remapped.shape[0], mu_local * aux_local)
    sigma_dev = sigma_total // n_dep
    summed = lax.psum_scatter(
        lax.dot_general(
            density_all, flattened, (((0,), (0,)), ((), ())), preferred_element_type=jnp.float32
        ).astype(jnp.bfloat16),
        "depth",
        scatter_dimension=0,
        tiled=True,
    ).astype(jnp.float32)
    return summed.reshape(sigma_dev, mu_local, aux_local).astype(jnp.bfloat16)


def solution(mesh):
    placed = (P(("row", "col", "depth"), None, None), P(("row", "col", "depth"), None), P(), P())
    return jax.shard_map(
        body, mesh=mesh, in_specs=placed, out_specs=P("depth", "row", "col"), check_vma=False
    )
```

profile of v0, /device:TPU:1, one launch (start us, length us, event | category | flops | bytes accessed | tf_op | source)
XLA Modules:
  0.0 481.7 jit_solution(15140523295629461933)
XLA Ops:
  6.5 1.1 copy.16
  7.7 21.2 %broadcast_in_dim.9 = s32[64,64,2,32]{2,1,0,3:T(8,128)} broadcast(s32[64,2,32]{1,0,2:T(8,128)S(1)} %copy.16), dimensions={0,2,3} | broadcast | bytes 1064960 | tf_op jit(solution)/shard_map/broadcast_in_dim | solution.py:14
  28.9 1.0 dynamic-slice_convert_fusion
  29.8 12.2 %mul.37 = bf16[16,2,64,32,64]{2,1,0,4,3:T(2,128)(2,1)} broadcast(bf16[16,2,32]{1,0,2:T(8,128)(2,1)S(1)} %dynamic-slice_convert_fusion), dimensions={0,1,3} | broadcast | bytes 8390656 | tf_op jit(solution)/shard_map/mul | solution.py:16
  42.0 27.0 %mul.38 = bf16[16,128,2048]{1,0,2:T(8,128)(2,1)} reshape(bf16[16,2,64,32,64]{2,1,0,4,3:T(2,128)(2,1)} %mul.37) | data formatting | bytes 16777216 | tf_op jit(solution)/shard_map/mul | solution.py:16
  69.0 12.5 %copy.17 = bf16[16,128,2048]{1,0,2:T(8,128)(2,1)} copy(bf16[16,128,2048]{2,1,0:T(8,128)(2,1)} %param.4) | data formatting | bytes 16777216 | tf_op args[0]
  81.5 9.6 %mul.39 = bf16[16,128,2048]{1,0,2:T(8,128)(2,1)} multiply(bf16[16,128,2048]{1,0,2:T(8,128)(2,1)} %copy.17, bf16[16,128,2048]{1,0,2:T(8,128)(2,1)} %mul.38) | non-fusion elementwise | flops 4194304 | bytes 25165824 | tf_op jit(solution)/shard_map/mul | solution.py:16
  91.1 0.0 copy-start.1
  91.1 0.0 copy-start
  91.1 7.8 %all-to-all-start = ((bf16[16,128,2048]{1,0,2:T(8,128)(2,1)}), bf16[16,128,2048]{1,0,2:T(8,128)(2,1)}, u32[]{:S(2)}, u32[]{:S(2)}) async-start(bf16[16,128,2048]{1,0,2:T(8,128)(2,1)} %mul.39), calls=%async_computation | async-start | bytes 16777216 | tf_op jit(solution)/shard_map/all_to_all | solution.py:27
  98.8 0.0 all-gather.2.cloned.1.call-start
  98.9 0.0 copy-done.1
  98.9 0.1 copy.15
  99.0 0.1 broadcast_in_dim.8
  99.1 0.1 mul.34
  99.2 0.1 mul.35
  99.4 0.0 copy-done
  99.4 0.6 mul.36
  100.0 0.0 all-gather.2.cloned.1.call-update
  100.0 0.0 reduce-scatter.2.cloned.1.call-start
  100.1 123.8 %all-to-all-done = bf16[16,128,2048]{1,0,2:T(8,128)(2,1)} async-done(((bf16[16,128,2048]{1,0,2:T(8,128)(2,1)}), bf16[16,128,2048]{1,0,2:T(8,128)(2,1)}, u32[]{:S(2)}, u32[]{:S(2)}) %all-to-all-start) | async-done | bytes 8388640 | tf_op jit(solution)/shard_map/all_to_all | solution.py:27
  223.9 12.9 %copy.19 = bf16[16,16,128,128]{3,2,1,0:T(8,128)(2,1)} copy(bf16[16,16,128,128]{2,1,3,0:T(8,128)(2,1)} %bitcast.4) | data formatting | bytes 16777216 | tf_op jit(solution)/shard_map/all_to_all | solution.py:27
  236.8 12.0 %copy.20 = bf16[256,128,128]{2,0,1:T(8,128)(2,1)} copy(bf16[256,128,128]{2,1,0:T(8,128)(2,1)} %bitcast.18) | data formatting | bytes 16777216 | tf_op jit(solution)/shard_map/all_to_all | solution.py:27
  248.8 20.4 %all_to_all.33 = bf16[256,128,128]{2,0,1:T(8,128)(2,1)} all-to-all(bf16[256,128,128]{2,0,1:T(8,128)(2,1)} %copy.20), channel_id=1, replica_groups=mesh['row'=2,'col'=16,'depth'=8] {'row'}, dimensions={1} | all-to-all | bytes 16777216 | tf_op jit(solution)/shard_map/all_to_all | solution.py:28
  269.2 12.0 %copy.21 = bf16[256,2,64,128]{3,2,0,1:T(8,128)(2,1)} copy(bf16[256,2,64,128]{3,0,2,1:T(8,128)(2,1)} %bitcast.19) | data formatting | bytes 16777216 | tf_op jit(solution)/shard_map/all_to_all | solution.py:28
  281.2 0.0 all-gather.2.cloned.1.call-done
  281.2 15.1 %convolution_convert_fusion = bf16[1024,8192]{1,0:T(8,128)(2,1)} fusion(bf16[512,1024]{1,0:T(8,128)(2,1)} %all-gather.2.cloned.1.call-done, bf16[64,8,64,128]{3,2,1,0:T(8,128)(2,1)} %bitcast.20), kind=kOutput, calls=%fused_computation | convolution fusion | flops 8598323200 | bytes 26214400 | tf_op jit(solution)/shard_map/dot_general | solution.py:34
  296.3 0.0 reduce-scatter.2.cloned.1.call-update
  296.3 175.1 %reduce-scatter.2.cloned.1.call-done = bf16[128,8192]{1,0:T(8,128)(2,1)} async-done(((bf16[1024,8192]{1,0:T(8,128)(2,1)}), bf16[128,8192]{1,0:T(8,128)(2,1)}) %reduce-scatter.2.cloned.1.call-update) | async-done | bytes 2097168 | tf_op jit(solution)/shard_map/reduce_scatter | solution.py:33
  471.4 3.5 copy.24
  (1 shorter events, 0.0 us)
Async XLA Ops:
  91.1 7.8 %copy-start.1 = (s32[64,16]{0,1:T(8,128)S(1)}, s32[64,16]{0,1:T(8,128)}, u32[]{:S(2)}) copy-start(s32[64,16]{0,1:T(8,128)} %param.7) | copy-start | bytes 12292
  91.1 8.3 %copy-start = (bf16[16,1024]{1,0:T(8,128)(2,1)S(1)}, bf16[16,1024]{1,0:T(8,128)(2,1)}, u32[]{:S(2)}) copy-start(bf16[16,1024]{1,0:T(8,128)(2,1)} %param.5) | copy-start | bytes 98308
  91.1 132.8 %all-to-all-start = ((bf16[16,128,2048]{1,0,2:T(8,128)(2,1)}), bf16[16,128,2048]{1,0,2:T(8,128)(2,1)}, u32[]{:S(2)}, u32[]{:S(2)}) async-start(bf16[16,128,2048]{1,0,2:T(8,128)(2,1)} %mul.39), calls=%async_computation | async-start | bytes 16777216 | tf_op jit(solution)/shard_map/all_to_all | solution.py:27
  98.8 182.4 %all-gather.2.cloned.1.call-start = ((), (), s32[]{:S(2)}) async-start(), calls=%async_computation.3 | async-start | bytes 1081344 | tf_op jit(solution)/shard_map/all_gather | solution.py:26
  100.0 371.3 %reduce-scatter.2.cloned.1.call-start = ((), (), s32[]{:S(2)}) async-start(), calls=%async_computation.4 | async-start | bytes 18874368 | tf_op jit(solution)/shard_map/reduce_scatter | solution.py:33
Sparse Core Ops, SparseCore 0:
  102.3 128.7 all-gather.1
  296.4 174.8 reduce-scatter.1
where the time goes:
time: 484 us; the launch traced here: 482 us
  waiting for transfers between devices  299 us (62%)
  local copies, waits for them, and re-layouts  115 us (24%)
  blocking collectives  20.4 us (4%)
  matrix products  15.1 us (3%)
  between operations  13.5 us (3%)
  other arithmetic  11.2 us (2%)
  starting transfers between devices  7.85 us (2%)
    reduce_scatter x1, waiting for transfers between devices, body(): lax.psum_scatter(lax.dot_general(density_all, flattened, (((0,), (0,)), (...  175 us
    all_to_all x1, waiting for transfers between devices, body(): lax.all_to_all(tensor_kept, 'col', split_axis=2, concat_axis=0, tiled=True)  124 us
    mul x2, local copies, waits for them, and re-layouts, body(): shaped * row_keep[:, :, None, :, None].astype(tensor.dtype)  39.1 us
    all_to_all x2, local copies, waits for them, and re-layouts, body(): lax.all_to_all(tensor_kept, 'col', split_axis=2, concat_axis=0, tiled=True)  24.9 us
    broadcast_in_dim x1, local copies, waits for them, and re-layouts, body(): jnp.repeat(tensor_mask, BLK, axis=0)  21.2 us
    all_to_all x1, blocking collectives, body(): lax.all_to_all(by_aux, 'row', split_axis=1, concat_axis=0, tiled=True)  20.4 us
    unnamed x8, local copies, waits for them, and re-layouts  17.3 us
    dot_general x1, matrix products, body(): lax.dot_general(density_all, flattened, (((0,), (0,)), ((), ())), preferr...  15.1 us
  transfers between devices with their start and end apart: 3, of which 2 were waited for; matrix products, arithmetic and copies ran while one was open for 8% of the time, Pallas kernels for 0%

commit v1 on v0

--- a/solution.py
+++ b/solution.py
@@ -25,7 +25,10 @@
     ).reshape(nu_dev, sigma_total)
     density_all = lax.all_gather(density_kept, ("row", "col"), axis=0, tiled=True)
     by_aux = lax.all_to_all(tensor_kept, "col", split_axis=2, concat_axis=0, tiled=True)
-    remapped = lax.all_to_all(by_aux, "row", split_axis=1, concat_axis=0, tiled=True)
+    remapped = jnp.concatenate(
+        lax.all_to_all(jnp.stack(jnp.split(by_aux, lax.axis_size("row"), axis=1)), "row", 0, 0),
+        axis=0,
+    )
     mu_local = remapped.shape[1]
     aux_local = remapped.shape[2]
     flattened = remapped.reshape(remapped.shape[0], mu_local * aux_local)

time: 484 us -> 467 us (0.965)
  blocking collectives: 20.4 us -> 0 us
  local copies, waits for them, and re-layouts: 115 us -> 96.6 us
  starting transfers between devices: 7.85 us -> 17 us
  waiting for transfers between devices: 299 us -> 306 us
  other arithmetic: 11.2 us -> 17.4 us
    all_to_all x1 -> x0, blocking collectives: 20.4 us -> none  [body(): lax.all_to_all(by_aux, 'row', split_axis=1, concat_axis=0, tiled=True)]
    all_to_all x2 -> x1, local copies, waits for them, and re-layouts: 24.9 us -> 12.9 us  [body(): lax.all_to_all(tensor_kept, 'col', split_axis=2, concat_axis=0, tiled=True)]
    all_to_all x1 -> x0, local copies, waits for them, and re-layouts: 12 us -> none  [body(): lax.all_to_all(by_aux, 'row', split_axis=1, concat_axis=0, tiled=True)]
    all_to_all x0 -> x1, starting transfers between devices: none -> 9.16 us  [body(): lax.all_to_all(jnp.stack(jnp.split(by_aux, lax.axis_size('row'), axis=1))...]
    all_to_all x0 -> x1, waiting for transfers between devices: none -> 7.12 us  [body(): lax.all_to_all(jnp.stack(jnp.split(by_aux, lax.axis_size('row'), axis=1))...]
    another operation x0 -> x1, other arithmetic: none -> 6.17 us  [body(): jnp.stack(jnp.split(by_aux, lax.axis_size('row'), axis=1))]
    another operation x0 -> x1, local copies, waits for them, and re-layouts: none -> 5.84 us  [body(): jnp.stack(jnp.split(by_aux, lax.axis_size('row'), axis=1))]
  transfers between devices with their start and end apart: 3 -> 4, of which waited for: 2 -> 3; matrix products, arithmetic and copies ran while one was open for 8% -> 6% of each run, Pallas kernels for 0% -> 0%
where the time goes in v1:
time: 467 us; the launch traced here: 466 us
  waiting for transfers between devices  306 us (66%)
  local copies, waits for them, and re-layouts  96.6 us (21%)
  other arithmetic  17.4 us (4%)
  starting transfers between devices  17 us (4%)
  matrix products  15.2 us (3%)
  between operations  13.5 us (3%)
    reduce_scatter x1, waiting for transfers between devices, body(): lax.psum_scatter(lax.dot_general(density_all, flattened, (((0,), (0,)), (...  175 us
    all_to_all x1, waiting for transfers between devices, body(): lax.all_to_all(tensor_kept, 'col', split_axis=2, concat_axis=0, tiled=True)  124 us
    mul x2, local copies, waits for them, and re-layouts, body(): shaped * row_keep[:, :, None, :, None].astype(tensor.dtype)  39.1 us
    broadcast_in_dim x1, local copies, waits for them, and re-layouts, body(): jnp.repeat(tensor_mask, BLK, axis=0)  21.2 us
    unnamed x8, local copies, waits for them, and re-layouts  17.3 us
    dot_general x1, matrix products, body(): lax.dot_general(density_all, flattened, (((0,), (0,)), ((), ())), preferr...  15.2 us
    all_to_all x1, local copies, waits for them, and re-layouts, body(): lax.all_to_all(tensor_kept, 'col', split_axis=2, concat_axis=0, tiled=True)  12.9 us
    mul x1, other arithmetic, body(): shaped * row_keep[:, :, None, :, None].astype(tensor.dtype)  9.57 us
  transfers between devices with their start and end apart: 4, of which 3 were waited for; matrix products, arithmetic and copies ran while one was open for 6% of the time, Pallas kernels for 0%

profile of v1, /device:TPU:1, one launch (start us, length us, event | category | flops | bytes accessed | tf_op | source)
XLA Modules:
  0.0 465.7 jit_solution(11287757119253870426)
XLA Ops:
  6.5 1.1 copy.14
  7.7 21.2 %broadcast_in_dim.9 = s32[64,64,2,32]{2,1,0,3:T(8,128)} broadcast(s32[64,2,32]{1,0,2:T(8,128)S(1)} %copy.14), dimensions={0,2,3} | broadcast | bytes 1064960 | tf_op jit(solution)/shard_map/broadcast_in_dim | solution.py:14
  28.9 1.0 dynamic-slice_convert_fusion
  29.8 12.2 %mul.37 = bf16[16,2,64,32,64]{2,1,0,4,3:T(2,128)(2,1)} broadcast(bf16[16,2,32]{1,0,2:T(8,128)(2,1)S(1)} %dynamic-slice_convert_fusion), dimensions={0,1,3} | broadcast | bytes 8390656 | tf_op jit(solution)/shard_map/mul | solution.py:16
  42.0 27.0 %mul.38 = bf16[16,128,2048]{1,0,2:T(8,128)(2,1)} reshape(bf16[16,2,64,32,64]{2,1,0,4,3:T(2,128)(2,1)} %mul.37) | data formatting | bytes 16777216 | tf_op jit(solution)/shard_map/mul | solution.py:16
  69.0 12.5 %copy.15 = bf16[16,128,2048]{1,0,2:T(8,128)(2,1)} copy(bf16[16,128,2048]{2,1,0:T(8,128)(2,1)} %param.4) | data formatting | bytes 16777216 | tf_op args[0]
  81.5 9.6 %mul.39 = bf16[16,128,2048]{1,0,2:T(8,128)(2,1)} multiply(bf16[16,128,2048]{1,0,2:T(8,128)(2,1)} %copy.15, bf16[16,128,2048]{1,0,2:T(8,128)(2,1)} %mul.38) | non-fusion elementwise | flops 4194304 | bytes 25165824 | tf_op jit(solution)/shard_map/mul | solution.py:16
  91.1 0.0 copy-start.1
  91.1 0.0 copy-start
  91.1 7.8 %all-to-all-start = ((bf16[16,128,2048]{1,0,2:T(8,128)(2,1)}), bf16[16,128,2048]{1,0,2:T(8,128)(2,1)}, u32[]{:S(2)}, u32[]{:S(2)}) async-start(bf16[16,128,2048]{1,0,2:T(8,128)(2,1)} %mul.39), calls=%async_computation | async-start | bytes 16777216 | tf_op jit(solution)/shard_map/all_to_all | solution.py:27
  98.8 0.0 all-gather.2.cloned.1.call-start
  98.9 0.0 copy-done.1
  98.9 0.1 copy.13
  99.0 0.1 broadcast_in_dim.8
  99.1 0.1 mul.34
  99.2 0.1 mul.35
  99.4 0.0 copy-done
  99.4 0.6 mul.36
  100.0 0.0 all-gather.2.cloned.1.call-update
  100.0 123.9 %all-to-all-done = bf16[16,128,2048]{1,0,2:T(8,128)(2,1)} async-done(((bf16[16,128,2048]{1,0,2:T(8,128)(2,1)}), bf16[16,128,2048]{1,0,2:T(8,128)(2,1)}, u32[]{:S(2)}, u32[]{:S(2)}) %all-to-all-start) | async-done | bytes 8388640 | tf_op jit(solution)/shard_map/all_to_all | solution.py:27
  223.9 12.9 %copy.17 = bf16[16,16,128,128]{3,2,1,0:T(8,128)(2,1)} copy(bf16[16,16,128,128]{2,1,3,0:T(8,128)(2,1)} %bitcast.4) | data formatting | bytes 16777216 | tf_op jit(solution)/shard_map/all_to_all | solution.py:27
  236.8 5.8 %slice_bitcast_fusion.1 = (bf16[1,256,64,128]{3,2,1,0:T(8,128)(2,1)S(1)}, bf16[1,256,64,128]{3,2,1,0:T(8,128)(2,1)}) fusion(bf16[256,128,128]{2,1,0:T(8,128)(2,1)} %bitcast.20), kind=kLoop, calls=%fused_computation.5 | loop fusion | bytes 16777216 | tf_op jit(solution)/shard_map/stack | solution.py:29
  242.6 6.2 %pad_maximum_fusion = bf16[2,256,64,128]{3,2,1,0:T(8,128)(2,1)} fusion(bf16[1,256,64,128]{3,2,1,0:T(8,128)(2,1)} %get-tuple-element.6, bf16[1,256,64,128]{3,2,1,0:T(8,128)(2,1)S(1)} %get-tuple-element.5), kind=kLoop, calls=%fused_computation.3 | loop fusion | flops 4194304 | bytes 16777216 | tf_op jit(solution)/shard_map/stack | solution.py:29
  248.8 9.2 %all-to-all-start.1 = ((bf16[2,256,64,128]{3,2,1,0:T(8,128)(2,1)}), bf16[2,256,64,128]{3,2,1,0:T(8,128)(2,1)}, u32[]{:S(2)}, u32[]{:S(2)}) async-start(bf16[2,256,64,128]{3,2,1,0:T(8,128)(2,1)} %pad_maximum_fusion), calls=%async_computation.1 | async-start | bytes 16777216 | tf_op jit(solution)/shard_map/all_to_all | solution.py:29
  257.9 0.0 reduce-scatter.2.cloned.1.call-start
  258.0 0.0 all-gather.2.cloned.1.call-done
  258.0 7.1 %all-to-all-done.1 = bf16[2,256,64,128]{3,2,1,0:T(8,128)(2,1)} async-done(((bf16[2,256,64,128]{3,2,1,0:T(8,128)(2,1)}), bf16[2,256,64,128]{3,2,1,0:T(8,128)(2,1)}, u32[]{:S(2)}, u32[]{:S(2)}) %all-to-all-start.1) | async-done | bytes 8388640 | tf_op jit(solution)/shard_map/all_to_all | solution.py:29
  265.1 15.2 %convolution_convert_fusion = bf16[1024,8192]{1,0:T(8,128)(2,1)} fusion(bf16[512,1024]{1,0:T(8,128)(2,1)} %all-gather.2.cloned.1.call-done, bf16[64,8,64,128]{3,2,1,0:T(8,128)(2,1)} %bitcast.10), kind=kOutput, calls=%fused_computation | convolution fusion | flops 8598323200 | bytes 26214400 | tf_op jit(solution)/shard_map/dot_general | solution.py:37
  280.2 0.0 reduce-scatter.2.cloned.1.call-update
  280.3 175.1 %reduce-scatter.2.cloned.1.call-done = bf16[128,8192]{1,0:T(8,128)(2,1)} async-done(((bf16[1024,8192]{1,0:T(8,128)(2,1)}), bf16[128,8192]{1,0:T(8,128)(2,1)}) %reduce-scatter.2.cloned.1.call-update) | async-done | bytes 2097168 | tf_op jit(solution)/shard_map/reduce_scatter | solution.py:36
  455.4 3.5 copy.20
  (1 shorter events, 0.0 us)
Async XLA Ops:
  91.1 7.8 %copy-start.1 = (s32[64,16]{0,1:T(8,128)S(1)}, s32[64,16]{0,1:T(8,128)}, u32[]{:S(2)}) copy-start(s32[64,16]{0,1:T(8,128)} %param.7) | copy-start | bytes 12292
  91.1 8.3 %copy-start = (bf16[16,1024]{1,0:T(8,128)(2,1)S(1)}, bf16[16,1024]{1,0:T(8,128)(2,1)}, u32[]{:S(2)}) copy-start(bf16[16,1024]{1,0:T(8,128)(2,1)} %param.5) | copy-start | bytes 98308
  91.1 132.8 %all-to-all-start = ((bf16[16,128,2048]{1,0,2:T(8,128)(2,1)}), bf16[16,128,2048]{1,0,2:T(8,128)(2,1)}, u32[]{:S(2)}, u32[]{:S(2)}) async-start(bf16[16,128,2048]{1,0,2:T(8,128)(2,1)} %mul.39), calls=%async_computation | async-start | bytes 16777216 | tf_op jit(solution)/shard_map/all_to_all | solution.py:27
  98.8 159.1 %all-gather.2.cloned.1.call-start = ((), (), s32[]{:S(2)}) async-start(), calls=%async_computation.3 | async-start | bytes 1081344 | tf_op jit(solution)/shard_map/all_gather | solution.py:26
  248.8 16.3 %all-to-all-start.1 = ((bf16[2,256,64,128]{3,2,1,0:T(8,128)(2,1)}), bf16[2,256,64,128]{3,2,1,0:T(8,128)(2,1)}, u32[]{:S(2)}, u32[]{:S(2)}) async-start(bf16[2,256,64,128]{3,2,1,0:T(8,128)(2,1)} %pad_maximum_fusion), calls=%async_computation.1 | async-start | bytes 16777216 | tf_op jit(solution)/shard_map/all_to_all | solution.py:29
  257.9 197.4 %reduce-scatter.2.cloned.1.call-start = ((), (), s32[]{:S(2)}) async-start(), calls=%async_computation.4 | async-start | bytes 18874368 | tf_op jit(solution)/shard_map/reduce_scatter | solution.py:36
Sparse Core Ops, SparseCore 0:
  102.3 128.7 all-gather.1
  280.4 174.9 reduce-scatter.1
